TPU v7x, 32 devices: a whole 2x2x4 slice. The times are simulated.
32 devices in a mesh: ta: 4 (over z), gx: 4 (over y, core), yz: 2 (over x).
Axes of the slice: x: 2, y: 2, z: 4, core: 2. Of those that a mesh axis runs over, the one named last changes fastest.
Arguments:
- source: float32 [2, 4, 3, 2, 8, 8, 8, 128], P(None, None, None, None, 'ta', 'gx', 'yz'), may hold values from -6 to 6
- gauge_links: float32 [2, 4, 3, 3, 8, 8, 8, 128], P(None, None, None, None, 'ta', 'gx', 'yz'), may hold values from -1 to 1, as said below
- photon_angles: float32 [4, 8, 8, 8, 128], P(None, 'ta', 'gx', 'yz'), may hold values from -3.140625 to 3.140625
Outputs:
- color_force: float32 [2, 4, 3, 3, 8, 8, 8, 128], P(None, None, None, None, 'ta', 'gx', 'yz')
- photon_force: float32 [4, 8, 8, 8, 128], P(None, 'ta', 'gx', 'yz')
Inputs may be any that keep to these rules, and one draw needn't show every extreme that they name: `gauge_links`: every 3x3 link matrix is unitary with determinant one.
All inputs are finite; a program needn't handle non-finite values.
Results may differ from a plain program's by a relative error of at most 0.0001.
Values sent between devices are 32-bit elements; how exact they have to be, the bound alone decides.
A program may use at most 128 MiB of HBM per device.

v0:
```python
import functools

import jax
import jax.numpy as jnp
from jax import lax
from jax.experimental import pallas as pl
from jax.experimental.pallas import tpu as pltpu
from jax.sharding import PartitionSpec as P

DEGREE = 4
HOPPING = 0.15
CHARGE = 2.0 / 3.0
MESH = pl.DeviceIdType.MESH

A_MATRIX = (
    ((0, 2), (1, 2)),
    ((1, 3), (0, 3)),
    ((1, 2), (0, 0)),
    ((0, 3), (1, 1)),
)
A_DAGGER = (
    ((0, 2), (1, 2)),
    ((1, 1), (0, 1)),
    ((1, 0), (0, 2)),
    ((0, 1), (1, 3)),
)


def add_phase(u, w, phase):
    phase = phase % 4
    if phase == 0:
        return (u[0] + w[0], u[1] + w[1])
    if phase == 1:
        return (u[0] - w[1], u[1] + w[0])
    if phase == 2:
        return (u[0] - w[0], u[1] - w[1])
    return (u[0] + w[1], u[1] - w[0])


def project(spinor, mu, plus):
    extra = 0 if plus else 2
    half = []
    for s in range(2):
        k, phase = A_MATRIX[mu][s]
        half.append([add_phase(spinor[s][a], spinor[2 + k][a], phase + extra) for a in range(3)])
    return half


def accumulate(total, half, mu, plus):
    extra = 0 if plus else 2
    out = []
    for s in range(2):
        out.append([add_phase(total[s][a], half[s][a], 0) for a in range(3)])
    for s in range(2):
        k, phase = A_DAGGER[mu][s]
        out.append([add_phase(total[2 + s][a], half[k][a], phase + extra) for a in range(3)])
    return out


def color_apply(link, half, dagger):
    out = []
    for s in range(2):
        rows = []
        for a in range(3):
            re = im = None
            for b in range(3):
                hr, hi = half[s][b]
                if dagger:
                    lr, li = link[b][a]
                    tr, ti = lr * hr + li * hi, lr * hi - li * hr
                else:
                    lr, li = link[a][b]
                    tr, ti = lr * hr - li * hi, lr * hi + li * hr
                re = tr if re is None else re + tr
                im = ti if im is None else im + ti
            rows.append((re, im))
        out.append(rows)
    return out


def map_half(fn, half):
    return [[(fn(h[0]), fn(h[1])) for h in row] for row in half]


def load_spinor(ref, c, t):
    return [[(ref[0, s, a, c, t], ref[1, s, a, c, t]) for a in range(3)] for s in range(4)]


def store_spinor(ref, c, t, values):
    for s in range(4):
        for a in range(3):
            ref[0, s, a, c, t] = values[s][a][0]
            ref[1, s, a, c, t] = values[s][a][1]


def load_half(ref, *where):
    return [[(ref[(0, s, a) + where], ref[(1, s, a) + where]) for a in range(3)] for s in range(2)]


def store_half(ref, half, *where):
    for s in range(2):
        for a in range(3):
            ref[(0, s, a) + where] = half[s][a][0]
            ref[(1, s, a) + where] = half[s][a][1]


def kernel(sizes, src, links, angles, force, photon, L, S, V, PX, send, recv, fsend, frecv,
           send_sem, recv_sem, fsend_sem, frecv_sem):
    copies, nt, nx, ny, nz = sizes
    R = nx * ny
    axes = ("ta", "gx", "yz")
    count = [lax.axis_size(a) for a in axes]
    here = [lax.axis_index(a) for a in axes]
    lower = [lax.rem(here[k] + count[k] - 1, count[k]) for k in range(3)]
    upper = [lax.rem(here[k] + 1, count[k]) for k in range(3)]

    def device(k, index):
        return tuple(index if j == k else here[j] for j in range(3))

    barrier = pltpu.get_barrier_semaphore()
    for k in range(3):
        for index in (lower[k], upper[k]):
            pl.semaphore_signal(barrier, inc=1, device_id=device(k, index), device_id_type=MESH)

    first = [(count[k] - here[k]) // count[k] for k in range(3)]
    last = [(here[k] + 1) // count[k] for k in range(3)]
    sign_ahead = (1 - 2 * first[0]).astype(jnp.float32)
    sign_behind = (1 - 2 * last[0]).astype(jnp.float32)
    row = lax.broadcasted_iota(jnp.int32, (R, nz), 0)
    row_x = row // ny
    row_y = row % ny

    for mu in range(4):
        def combine(t, carry):
            angle = CHARGE * angles[mu, t]
            cosine = HOPPING * jnp.cos(angle)
            sine = HOPPING * jnp.sin(angle)
            for a in range(3):
                for b in range(3):
                    re = links[0, mu, a, b, t]
                    im = links[1, mu, a, b, t]
                    L[0, mu, a, b, t] = cosine * re - sine * im
                    L[1, mu, a, b, t] = cosine * im + sine * re
            return carry

        lax.fori_loop(0, nt, combine, 0)

    def load_link(mu, c, t):
        sign = (1 - 2 * c).astype(jnp.float32)
        return [[(L[0, mu, a, b, t], L[1, mu, a, b, t] * sign) for b in range(3)] for a in range(3)]

    def items(body, times=nt):
        def step(i, carry):
            body(i % copies, i // copies)
            return carry

        lax.fori_loop(0, times * copies, step, 0)

    for group in (send[2:], fsend[1:]):
        for ref in group:
            ref[...] = jnp.zeros_like(ref)

    def start_field(c, t):
        values = load_spinor(src, c, t)
        store_spinor(S, c, t, values)
        store_spinor(V.at[0], c, t, values)

    items(start_field)

    def copy_of(kind, parity):
        k = kind // 2
        to = lower[k] if kind % 2 == 0 else upper[k]
        return pltpu.make_async_remote_copy(
            src_ref=send[kind], dst_ref=recv[kind].at[parity],
            send_sem=send_sem.at[kind], recv_sem=recv_sem.at[kind, parity],
            device_id=device(k, to), device_id_type=MESH)

    def force_copy(k):
        return pltpu.make_async_remote_copy(
            src_ref=fsend[k], dst_ref=frecv[k],
            send_sem=fsend_sem.at[k], recv_sem=frecv_sem.at[k],
            device_id=device(k, lower[k]), device_id_type=MESH)

    def slot_of(k, c, t, flip):
        if k == 1:
            i = t * copies + c + flip * (1 - 2 * c)
            return i // nx, i % nx
        i = t * copies + c
        return i // ny, i % ny

    def pack(ref, half, k, c, t, ahead):
        if k == 1:
            tile, slot = slot_of(1, c, t, first[1] if ahead else last[1])
            shift = slot * ny if ahead else (slot + 1) * ny
            mask = row_x == slot
        else:
            tile, slot = slot_of(2, c, t, 0)
            shift = slot if ahead else slot + 1 + R - ny
            mask = row_y == slot
        shift = lax.rem(shift, R)
        for s in range(2):
            for a in range(3):
                for ri in range(2):
                    moved = pltpu.roll(half[s][a][ri], shift, 0)
                    ref[ri, s, a, tile] = jnp.where(mask, moved, ref[ri, s, a, tile])

    def shifted(half, ref, k, c, t, ahead):
        tile, slot = slot_of(k, c, t, 0)
        if k == 1:
            own = R - ny if ahead else ny
            shift = (nx - 1 - slot) * ny if ahead else (nx - slot) * ny
            mask = row_x == (nx - 1 if ahead else 0)
        else:
            own = R - 1 if ahead else 1
            shift = ny - 1 - slot if ahead else R - slot
            mask = row_y == (ny - 1 if ahead else 0)
        shift = lax.rem(shift, R)
        out = []
        for s in range(2):
            line = []
            for a in range(3):
                line.append(tuple(
                    jnp.where(mask, pltpu.roll(ref[ri, s, a, tile], shift, 0),
                              pltpu.roll(half[s][a][ri], own, 0))
                    for ri in range(2)))
            out.append(line)
        return out

    def ahead_face_t(field, ref, plus):
        def body(c, t):
            half = project(load_spinor(field, c, 0), 0, plus)
            store_half(ref, map_half(lambda h: h * sign_ahead, half), c)
        items(body, 1)

    def z_ahead(half):
        return map_half(lambda h: pltpu.roll(h, nz - 1, 1), half)

    def z_behind(half):
        return map_half(lambda h: pltpu.roll(h, 1, 1), half)

    pl.semaphore_wait(barrier, 6)

    def hop(n, carry):
        parity = lax.rem(n, 2)
        now = V.at[parity]
        new = V.at[1 - parity]

        @pl.when(n == DEGREE)
        def _():
            def restart(c, t):
                values = load_spinor(now, c, t)
                values = values[:2] + map_half(lambda h: -h, values[2:])
                store_spinor(S, c, t, values)
                store_spinor(now, c, t, values)
            items(restart)

        def face_t(c, t):
            half = project(load_spinor(now, c, 0), 0, False)
            store_half(send[0], map_half(lambda h: h * sign_ahead, half), c)
            half = project(load_spinor(now, c, nt - 1), 0, True)
            half = color_apply(load_link(0, c, nt - 1), half, True)
            store_half(send[1], map_half(lambda h: h * sign_behind, half), c)

        items(face_t, 1)
        copy_of(0, parity).start()
        copy_of(1, parity).start()

        def face_xy(c, t):
            spinor = load_spinor(now, c, t)
            for k in (1, 2):
                pack(send[2 * k], project(spinor, k, False), k, c, t, True)
                half = color_apply(load_link(k, c, t), project(spinor, k, True), True)
                store_half(PX.at[k - 1], half, c, t)
                pack(send[2 * k + 1], half, k, c, t, False)

        items(face_xy)
        for kind in range(2, 6):
            copy_of(kind, parity).start()

        @pl.when(n == DEGREE)
        def _():
            ahead_face_t(S, fsend[0], True)

            def face(c, t):
                spinor = load_spinor(S, c, t)
                for k in (1, 2):
                    pack(fsend[k], project(spinor, k, True), k, c, t, True)
            items(face)
            for k in range(3):
                force_copy(k).start()

        def along_z(c, t):
            total = load_spinor(S, c, t)
            spinor = load_spinor(now, c, t)
            link = load_link(3, c, t)
            half = color_apply(link, project(spinor, 3, True), True)
            total = accumulate(total, z_behind(half), 3, True)
            half = color_apply(link, z_ahead(project(spinor, 3, False)), False)
            total = accumulate(total, half, 3, False)
            store_spinor(new, c, t, total)

        items(along_z)

        def along_t(c, t):
            link = load_link(0, c, t)
            half = color_apply(link, project(load_spinor(now, c, t + 1), 0, False), False)
            store_spinor(new, c, t, accumulate(load_spinor(new, c, t), half, 0, False))
            half = color_apply(link, project(load_spinor(now, c, t), 0, True), True)
            store_spinor(new, c, t + 1, accumulate(load_spinor(new, c, t + 1), half, 0, True))

        if nt > 1:
            items(along_t, nt - 1)

        for kind in range(2, 6):
            copy_of(kind, parity).wait_recv()

        def along_xy(c, t):
            spinor = load_spinor(now, c, t)
            total = load_spinor(new, c, t)
            for k in (1, 2):
                half = shifted(project(spinor, k, False), recv[2 * k].at[parity], k, c, t, True)
                half = color_apply(load_link(k, c, t), half, False)
                total = accumulate(total, half, k, False)
                half = load_half(PX.at[k - 1], c, t)
                half = shifted(half, recv[2 * k + 1].at[parity], k, c, t, False)
                total = accumulate(total, half, k, True)
            store_spinor(new, c, t, total)

        items(along_xy)

        for kind in range(2):
            copy_of(kind, parity).wait_recv()

        def edge_t(c, t):
            half = load_half(recv[0].at[parity], c)
            half = color_apply(load_link(0, c, nt - 1), half, False)
            total = load_spinor(new, c, nt - 1)
            store_spinor(new, c, nt - 1, accumulate(total, half, 0, False))
            half = load_half(recv[1].at[parity], c)
            store_spinor(new, c, 0, accumulate(load_spinor(new, c, 0), half, 0, True))

        items(edge_t, 1)
        for kind in range(6):
            copy_of(kind, parity).wait_send()
        return carry

    lax.fori_loop(0, 2 * DEGREE, hop, 0)

    W = V.at[0]
    ahead_face_t(W, send[0], False)
    copy_of(0, 0).start()

    def last_face(c, t):
        spinor = load_spinor(W, c, t)
        for k in (1, 2):
            pack(send[2 * k], project(spinor, k, False), k, c, t, True)

    items(last_face)
    copy_of(2, 0).start()
    copy_of(4, 0).start()

    def outer_into(out, left, right):
        for a in range(3):
            for b in range(3):
                for s in range(2):
                    lr, li = left[s][a]
                    rr, ri = right[s][b]
                    re = lr * rr + li * ri
                    im = li * rr - lr * ri
                    old = out[a][b]
                    out[a][b] = (re, im) if old is None else (old[0] + re, old[1] + im)
        return out

    def finish(mu, t, heads):
        both = None
        for c in range(copies):
            ahead_x, ahead_y = heads(c)
            here_y = project(load_spinor(W, c, t), mu, True)
            here_x = project(load_spinor(S, c, t), mu, False)
            out = [[None] * 3 for _ in range(3)]
            out = outer_into(out, ahead_x, here_y)
            out = outer_into(out, ahead_y, here_x)
            if both is None:
                both = out
            else:
                both = [[(both[a][b][0] + out[a][b][0], both[a][b][1] - out[a][b][1])
                         for b in range(3)] for a in range(3)]
        merged = []
        for a in range(3):
            line = []
            for b in range(3):
                re = im = None
                for k in range(3):
                    lr, li = L[0, mu, a, k, t], L[1, mu, a, k, t]
                    br, bi = both[k][b]
                    tr, ti = lr * br - li * bi, lr * bi + li * br
                    re = tr if re is None else re + tr
                    im = ti if im is None else im + ti
                line.append((re, im))
            merged.append(line)
        trace = merged[0][0][1] + merged[1][1][1] + merged[2][2][1]
        third = trace * (1.0 / 3.0)
        photon[mu, t] = CHARGE * trace
        for a in range(3):
            force[0, mu, a, a, t] = jnp.zeros_like(trace)
            force[1, mu, a, a, t] = merged[a][a][1] - third
            for b in range(a + 1, 3):
                re = 0.5 * (merged[a][b][0] - merged[b][a][0])
                im = 0.5 * (merged[a][b][1] + merged[b][a][1])
                force[0, mu, a, b, t] = re
                force[0, mu, b, a, t] = -re
                force[1, mu, a, b, t] = im
                force[1, mu, b, a, t] = im

    def over_t(body, times=nt):
        def step(t, carry):
            body(t)
            return carry
        lax.fori_loop(0, times, step, 0)

    def force_z(t):
        finish(3, t, lambda c: (z_ahead(project(load_spinor(S, c, t), 3, True)),
                                z_ahead(project(load_spinor(W, c, t), 3, False))))

    over_t(force_z)

    def force_t(t):
        finish(0, t, lambda c: (project(load_spinor(S, c, t + 1), 0, True),
                                project(load_spinor(W, c, t + 1), 0, False)))

    if nt > 1:
        over_t(force_t, nt - 1)

    for k in (2, 1, 0):
        force_copy(k).wait()
        copy_of(2 * k, 0).wait()
        if k == 0:
            finish(0, nt - 1, lambda c: (load_half(frecv[0], c), load_half(recv[0].at[0], c)))
        else:
            def force_k(t):
                finish(k, t, lambda c: (
                    shifted(project(load_spinor(S, c, t), k, True), frecv[k], k, c, t, True),
                    shifted(project(load_spinor(W, c, t), k, False), recv[2 * k].at[0], k, c, t,
                            True)))
            over_t(force_k)


def per_device(source, gauge_links, photon_angles):
    _, _, _, copies, nt, nx, ny, nz = source.shape
    R = nx * ny
    total = copies * nt
    face = [(2, 2, 3, copies, R, nz),
            (2, 2, 3, -(-total // nx), R, nz),
            (2, 2, 3, -(-total // ny), R, nz)]
    f32 = jnp.float32
    field = (2, 4, 3, copies, nt, R, nz)

    def vm(shape):
        return pltpu.VMEM(shape, f32)

    color, photon = pl.pallas_call(
        functools.partial(kernel, (copies, nt, nx, ny, nz)),
        out_shape=(jax.ShapeDtypeStruct((2, 4, 3, 3, nt, R, nz), f32),
                   jax.ShapeDtypeStruct((4, nt, R, nz), f32)),
        in_specs=[pl.BlockSpec(memory_space=pltpu.VMEM)] * 3,
        out_specs=(pl.BlockSpec(memory_space=pltpu.VMEM),) * 2,
        scratch_shapes=[
            vm((2, 4, 3, 3, nt, R, nz)),
            vm(field),
            vm((2,) + field),
            vm((2, 2, 2, 3, copies, nt, R, nz)),
            [vm(face[kind // 2]) for kind in range(6)],
            [vm((2,) + face[kind // 2]) for kind in range(6)],
            [vm(face[k]) for k in range(3)],
            [vm(face[k]) for k in range(3)],
            pltpu.SemaphoreType.DMA((6,)),
            pltpu.SemaphoreType.DMA((6, 2)),
            pltpu.SemaphoreType.DMA((3,)),
            pltpu.SemaphoreType.DMA((3,)),
        ],
        compiler_params=pltpu.CompilerParams(
            collective_id=0, has_side_effects=True, vmem_limit_bytes=40 * 1024 * 1024),
    )(source.reshape(2, 4, 3, copies, nt, R, nz),
      gauge_links.reshape(2, 4, 3, 3, nt, R, nz),
      photon_angles.reshape(4, nt, R, nz))
    return (color.reshape(2, 4, 3, 3, nt, nx, ny, nz), photon.reshape(4, nt, nx, ny, nz))


def solution(mesh):
    in_specs = (
        P(None, None, None, None, "ta", "gx", "yz", None),
        P(None, None, None, None, "ta", "gx", "yz", None),
        P(None, "ta", "gx", "yz", None),
    )
    out_specs = (P(None, None, None, None, "ta", "gx", "yz", None), P(None, "ta", "gx", "yz", None))
    return jax.shard_map(
        per_device, mesh=mesh, in_specs=in_specs, out_specs=out_specs, check_vma=False
    )
```

profile of v0, /device:TPU:0, one launch (start us, length us, event | category | flops | bytes accessed | tf_op | source)
XLA Modules:
  0.0 62.8 jit_solution(3687834869127152909)
XLA Ops:
  0.6 0.0 copy-start
  0.6 1.1 %copy-done = f32[2,4,3,3,2,2,4,128]{7,6,5,4,3,2,1,0:T(4,128)S(1)} copy-done((f32[2,4,3,3,2,2,4,128]{7,6,5,4,3,2,1,0:T(4,128)S(1)}, f32[2,4,3,3,2,2,4,128]{7,6,5,4,3,2,1,0:T(4,128)}, u32[]{:S(2)}) %copy-start) | copy-done | bytes 589848
  1.7 0.0 copy-start.1
  1.7 1.0 %copy-done.1 = f32[2,4,3,2,2,2,4,128]{7,6,5,4,3,2,1,0:T(4,128)S(1)} copy-done((f32[2,4,3,2,2,2,4,128]{7,6,5,4,3,2,1,0:T(4,128)S(1)}, f32[2,4,3,2,2,2,4,128]{7,6,5,4,3,2,1,0:T(4,128)}, u32[]{:S(2)}) %copy-start.1) | copy-done | bytes 393240
  2.7 0.0 copy-start.2
  2.7 0.8 %copy-done.2 = f32[4,2,2,4,128]{4,3,2,1,0:T(4,128)S(1)} copy-done((f32[4,2,2,4,128]{4,3,2,1,0:T(4,128)S(1)}, f32[4,2,2,4,128]{4,3,2,1,0:T(4,128)}, u32[]{:S(2)}) %copy-start.2) | copy-done | bytes 32792
  3.5 57.9 %shard_map.50 = (f32[2,4,3,3,2,8,128]{6,5,4,3,2,1,0:T(8,128)S(1)}, f32[4,2,8,128]{3,2,1,0:T(8,128)S(1)}) custom-call(f32[2,4,3,2,2,8,128]{6,5,4,3,2,1,0:T(8,128)S(1)} %bitcast.7, f32[2,4,3,3,2,8,128]{6,5,4,3,2,1,0:T(8,128)S(1)} %bitcast.5, f32[4,2,8,128]{3,2,1,0:T(8,128)S(1)} %bitcast.8), custom_call_target="tpu_custom_call" | custom-call | tf_op jit(solution)/shard_map/pallas_call | solution.py:461
  61.4 0.8 %copy.7 = f32[2,4,3,3,2,2,4,128]{7,6,5,4,3,2,1,0:T(4,128)} copy(f32[2,4,3,3,2,2,4,128]{7,6,5,4,3,2,1,0:T(4,128)S(1)} %bitcast.6) | data formatting | bytes 1179648
  62.2 0.6 copy.8
Async XLA Ops:
  0.6 1.1 %copy-start = (f32[2,4,3,3,2,2,4,128]{7,6,5,4,3,2,1,0:T(4,128)S(1)}, f32[2,4,3,3,2,2,4,128]{7,6,5,4,3,2,1,0:T(4,128)}, u32[]{:S(2)}) copy-start(f32[2,4,3,3,2,2,4,128]{7,6,5,4,3,2,1,0:T(4,128)} %param.4) | copy-start | bytes 1769476
  1.7 1.0 %copy-start.1 = (f32[2,4,3,2,2,2,4,128]{7,6,5,4,3,2,1,0:T(4,128)S(1)}, f32[2,4,3,2,2,2,4,128]{7,6,5,4,3,2,1,0:T(4,128)}, u32[]{:S(2)}) copy-start(f32[2,4,3,2,2,2,4,128]{7,6,5,4,3,2,1,0:T(4,128)} %param.3) | copy-start | bytes 1179652
  2.7 0.8 %copy-start.2 = (f32[4,2,2,4,128]{4,3,2,1,0:T(4,128)S(1)}, f32[4,2,2,4,128]{4,3,2,1,0:T(4,128)}, u32[]{:S(2)}) copy-start(f32[4,2,2,4,128]{4,3,2,1,0:T(4,128)} %param.5) | copy-start | bytes 98308
where the time goes:
time: 63.4 us; the launch traced here: 62.8 us
  Pallas kernels  57.9 us (91%)
  local copies, waits for them, and re-layouts  4.24 us (7%)
  between operations  0.65 us (1%)
    pallas_call x1, Pallas kernels, per_device(): pl.pallas_call(functools.partial(kernel, (copies, nt, nx, ny, nz)), out_s...  57.9 us
    unnamed x8, local copies, waits for them, and re-layouts  4.24 us

commit v1 on v0

v1 whole, which is shorter than its diff:
```python
import functools

import jax
import jax.numpy as jnp
from jax import lax
from jax.experimental import pallas as pl
from jax.experimental.pallas import tpu as pltpu
from jax.sharding import PartitionSpec as P

DEGREE = 4
HOPPING = 0.15
CHARGE = 2.0 / 3.0
MESH = pl.DeviceIdType.MESH

A_MATRIX = (
    ((0, 2), (1, 2)),
    ((1, 3), (0, 3)),
    ((1, 2), (0, 0)),
    ((0, 3), (1, 1)),
)
A_DAGGER = (
    ((0, 2), (1, 2)),
    ((1, 1), (0, 1)),
    ((1, 0), (0, 2)),
    ((0, 1), (1, 3)),
)


def add_phase(u, w, phase):
    phase = phase % 4
    if phase == 0:
        return (u[0] + w[0], u[1] + w[1])
    if phase == 1:
        return (u[0] - w[1], u[1] + w[0])
    if phase == 2:
        return (u[0] - w[0], u[1] - w[1])
    return (u[0] + w[1], u[1] - w[0])


def project(spinor, mu, plus):
    extra = 0 if plus else 2
    half = []
    for s in range(2):
        k, phase = A_MATRIX[mu][s]
        half.append([add_phase(spinor[s][a], spinor[2 + k][a], phase + extra) for a in range(3)])
    return half


def accumulate(total, half, mu, plus):
    extra = 0 if plus else 2
    out = []
    for s in range(2):
        out.append([add_phase(total[s][a], half[s][a], 0) for a in range(3)])
    for s in range(2):
        k, phase = A_DAGGER[mu][s]
        out.append([add_phase(total[2 + s][a], half[k][a], phase + extra) for a in range(3)])
    return out


def color_apply(link, half, dagger):
    out = []
    for s in range(2):
        rows = []
        for a in range(3):
            re = im = None
            for b in range(3):
                hr, hi = half[s][b]
                if dagger:
                    lr, li = link[b][a]
                    tr, ti = lr * hr + li * hi, lr * hi - li * hr
                else:
                    lr, li = link[a][b]
                    tr, ti = lr * hr - li * hi, lr * hi + li * hr
                re = tr if re is None else re + tr
                im = ti if im is None else im + ti
            rows.append((re, im))
        out.append(rows)
    return out


def map_half(fn, half):
    return [[(fn(h[0]), fn(h[1])) for h in row] for row in half]


def load_spinor(ref, t):
    return [[(ref[0, s, a, t], ref[1, s, a, t]) for a in range(3)] for s in range(4)]


def store_spinor(ref, t, values):
    for s in range(4):
        for a in range(3):
            ref[0, s, a, t] = values[s][a][0]
            ref[1, s, a, t] = values[s][a][1]


def load_half(ref, *where):
    return [[(ref[(0, s, a) + where], ref[(1, s, a) + where]) for a in range(3)] for s in range(2)]


def store_half(ref, half, *where):
    for s in range(2):
        for a in range(3):
            ref[(0, s, a) + where] = half[s][a][0]
            ref[(1, s, a) + where] = half[s][a][1]


def kernel(sizes, src, links, angles, force, photon, L, S, V, PX, send, recv, fsend, frecv,
           send_sem, recv_sem, fsend_sem, frecv_sem):
    copies, nt, nx, ny, nz = sizes
    R = nx * ny
    axes = ("ta", "gx", "yz")
    count = [lax.axis_size(a) for a in axes]
    here = [lax.axis_index(a) for a in axes]
    lower = [lax.rem(here[k] + count[k] - 1, count[k]) for k in range(3)]
    upper = [lax.rem(here[k] + 1, count[k]) for k in range(3)]

    def device(k, index):
        return tuple(index if j == k else here[j] for j in range(3))

    barrier = pltpu.get_barrier_semaphore()
    for k in range(3):
        for index in (lower[k], upper[k]):
            pl.semaphore_signal(barrier, inc=1, device_id=device(k, index), device_id_type=MESH)

    first = [(count[k] - here[k]) // count[k] for k in range(3)]
    last = [(here[k] + 1) // count[k] for k in range(3)]
    sign_ahead = (1 - 2 * first[0]).astype(jnp.float32)
    sign_behind = (1 - 2 * last[0]).astype(jnp.float32)
    row = lax.broadcasted_iota(jnp.int32, (R, nz), 0)
    row_x = row // ny
    row_y = row % ny

    lane = lax.broadcasted_iota(jnp.int32, (R, nz), 1)
    corner = here[0] * nt + here[1] * nx + here[2] * ny

    def even(t):
        return (corner + t + row_x + row_y + lane) % 2 == 0

    def merge(t, zero, one, p):
        mask = even(t)
        if p == 0:
            return jnp.where(mask, zero, one)
        return jnp.where(mask, one, zero)

    def over_t(body, times=nt):
        def step(t, carry):
            body(t)
            return carry

        lax.fori_loop(0, times, step, 0)

    for mu in range(4):
        def combine(t):
            angle = CHARGE * angles[mu, t]
            cosine = HOPPING * jnp.cos(angle)
            sine = HOPPING * jnp.sin(angle)
            for a in range(3):
                for b in range(3):
                    re = links[0, mu, a, b, t]
                    im = links[1, mu, a, b, t]
                    re, im = cosine * re - sine * im, cosine * im + sine * re
                    re_one, im_one = pltpu.roll(re, nz - 1, 1), -pltpu.roll(im, nz - 1, 1)
                    for p in range(2):
                        L[p, 0, mu, a, b, t] = merge(t, re, re_one, p)
                        L[p, 1, mu, a, b, t] = merge(t, im, im_one, p)

        over_t(combine)

    def load_link(p, mu, t):
        return [[(L[p, 0, mu, a, b, t], L[p, 1, mu, a, b, t]) for b in range(3)] for a in range(3)]

    for group in (send[2:], fsend[1:]):
        for ref in group:
            ref[...] = jnp.zeros_like(ref)

    def start_field(t):
        for s in range(4):
            for a in range(3):
                for ri in range(2):
                    zero = src[ri, s, a, 0, t]
                    one = pltpu.roll(src[ri, s, a, 1, t], nz - 1, 1)
                    for p in range(2):
                        value = merge(t, zero, one, p)
                        S[p, ri, s, a, t] = value
                        V[0, p, ri, s, a, t] = value

    over_t(start_field)

    def copy_of(kind, m):
        k = kind // 2
        to = lower[k] if kind % 2 == 0 else upper[k]
        chain, slot = lax.rem(m, 2), lax.rem(m, 4)
        return pltpu.make_async_remote_copy(
            src_ref=send[kind].at[chain], dst_ref=recv[kind].at[slot],
            send_sem=send_sem.at[kind, chain], recv_sem=recv_sem.at[kind, slot],
            device_id=device(k, to), device_id_type=MESH)

    def force_copy(k, p):
        return pltpu.make_async_remote_copy(
            src_ref=fsend[k].at[p], dst_ref=frecv[k].at[p],
            send_sem=fsend_sem.at[k, p], recv_sem=frecv_sem.at[k, p],
            device_id=device(k, lower[k]), device_id_type=MESH)

    def slot_of(k, ri, t):
        i = ri * nt + t
        return (i // nx, i % nx) if k == 1 else (i // ny, i % ny)

    def pack(ref, half, k, t, ahead):
        for ri in range(2):
            tile, slot = slot_of(k, ri, t)
            if k == 1:
                shift = slot * ny if ahead else (slot + 1) * ny
                mask = row_x == slot
            else:
                shift = slot if ahead else slot + 1 + R - ny
                mask = row_y == slot
            shift = lax.rem(shift, R)
            for s in range(2):
                for a in range(3):
                    moved = pltpu.roll(half[s][a][ri], shift, 0)
                    ref[s, a, tile] = jnp.where(mask, moved, ref[s, a, tile])

    def shifted(half, ref, k, p, t, ahead):
        out = [[[None, None] for a in range(3)] for s in range(2)]
        if k == 1:
            own = R - ny if ahead else ny
            mask = row_x == (nx - 1 if ahead else 0)
            wraps = (last[1] if ahead else first[1]) == 1
            copy_zero = (corner + t + row_x + row_y + lane + p) % 2 == 0
        else:
            own = R - 1 if ahead else 1
            mask = row_y == (ny - 1 if ahead else 0)
        for ri in range(2):
            tile, slot = slot_of(k, ri, t)
            if k == 1:
                shift = (nx - 1 - slot) * ny if ahead else (nx - slot) * ny
            else:
                shift = ny - 1 - slot if ahead else R - slot
            shift = lax.rem(shift, R)
            for s in range(2):
                for a in range(3):
                    face = pltpu.roll(ref[s, a, tile], shift, 0)
                    if k == 1:
                        other = jnp.where(copy_zero, pltpu.roll(face, 1, 1),
                                          pltpu.roll(face, nz - 1, 1))
                        face = jnp.where(wraps, other, face)
                    out[s][a][ri] = jnp.where(mask, face, pltpu.roll(half[s][a][ri], own, 0))
        return out

    def z_ahead(half):
        return map_half(lambda h: pltpu.roll(h, nz - 1, 1), half)

    def z_behind(half):
        return map_half(lambda h: pltpu.roll(h, 1, 1), half)

    def ahead_face_t(field, ref, plus):
        half = project(load_spinor(field, 0), 0, plus)
        store_half(ref, map_half(lambda h: h * sign_ahead, half))

    def send_faces(field, p, m, behind):
        chain = lax.rem(m, 2)
        ahead_face_t(field, send[0].at[chain], False)
        copy_of(0, m).start()

        def behind_t():
            half = project(load_spinor(field, nt - 1), 0, True)
            half = color_apply(load_link(p, 0, nt - 1), half, True)
            store_half(send[1].at[chain], map_half(lambda h: h * sign_behind, half))
            copy_of(1, m).start()

        pl.when(behind)(behind_t)

        def face_xy(t):
            spinor = load_spinor(field, t)
            for k in (1, 2):
                pack(send[2 * k].at[chain], project(spinor, k, False), k, t, True)
                half = color_apply(load_link(p, k, t), project(spinor, k, True), True)
                store_half(PX.at[chain, k - 1], half, t)
                pack(send[2 * k + 1].at[chain], half, k, t, False)

        over_t(face_xy)
        copy_of(2, m).start()
        copy_of(4, m).start()

        def behind_xy():
            copy_of(3, m).start()
            copy_of(5, m).start()

        pl.when(behind)(behind_xy)

    rounds = 2 * DEGREE
    pl.semaphore_wait(barrier, 6)

    def first_faces(m, carry):
        send_faces(V.at[0, m], m, m, m >= 0)
        return carry

    lax.fori_loop(0, 2, first_faces, 0)

    def hop(m, carry):
        n = m // 2
        chain = lax.rem(m, 2)
        slot = lax.rem(m, 4)
        p = lax.rem(chain + n, 2)
        q = 1 - p
        now = V.at[lax.rem(n, 2), p]
        new = V.at[lax.rem(n + 1, 2), q]

        def along_z(t):
            total = load_spinor(S.at[q], t)
            spinor = load_spinor(now, t)
            half = color_apply(load_link(p, 3, t), project(spinor, 3, True), True)
            total = accumulate(total, z_behind(half), 3, True)
            half = z_ahead(project(spinor, 3, False))
            half = color_apply(load_link(q, 3, t), half, False)
            total = accumulate(total, half, 3, False)
            store_spinor(new, t, total)

        over_t(along_z)

        def along_t(t):
            half = project(load_spinor(now, t + 1), 0, False)
            half = color_apply(load_link(q, 0, t), half, False)
            store_spinor(new, t, accumulate(load_spinor(new, t), half, 0, False))
            half = color_apply(load_link(p, 0, t), project(load_spinor(now, t), 0, True), True)
            store_spinor(new, t + 1, accumulate(load_spinor(new, t + 1), half, 0, True))

        if nt > 1:
            over_t(along_t, nt - 1)

        for kind in range(2, 6):
            copy_of(kind, m).wait_recv()

        def along_xy(t):
            spinor = load_spinor(now, t)
            total = load_spinor(new, t)
            for k in (1, 2):
                half = shifted(project(spinor, k, False), recv[2 * k].at[slot], k, q, t, True)
                half = color_apply(load_link(q, k, t), half, False)
                total = accumulate(total, half, k, False)
                half = load_half(PX.at[chain, k - 1], t)
                half = shifted(half, recv[2 * k + 1].at[slot], k, q, t, False)
                total = accumulate(total, half, k, True)
            store_spinor(new, t, total)

        over_t(along_xy)

        for kind in range(2):
            copy_of(kind, m).wait_recv()
        half = color_apply(load_link(q, 0, nt - 1), load_half(recv[0].at[slot]), False)
        total = accumulate(load_spinor(new, nt - 1), half, 0, False)
        store_spinor(new, nt - 1, total)
        half = load_half(recv[1].at[slot])
        store_spinor(new, 0, accumulate(load_spinor(new, 0), half, 0, True))
        for kind in range(6):
            copy_of(kind, m).wait_send()

        @pl.when(n == DEGREE - 1)
        def _():
            def restart(t):
                values = load_spinor(new, t)
                values = values[:2] + map_half(lambda h: -h, values[2:])
                store_spinor(S.at[q], t, values)
                store_spinor(new, t, values)

            over_t(restart)

        send_faces(new, q, m + 2, n < rounds - 1)

        @pl.when(n == DEGREE - 1)
        def _():
            ahead_face_t(S.at[q], fsend[0].at[q], True)

            def face(t):
                spinor = load_spinor(S.at[q], t)
                for k in (1, 2):
                    pack(fsend[k].at[q], project(spinor, k, True), k, t, True)

            over_t(face)
            for k in range(3):
                force_copy(k, q).start()

        return carry

    lax.fori_loop(0, 2 * rounds, hop, 0)

    W = V.at[rounds % 2]

    def outer_into(out, left, right):
        for a in range(3):
            for b in range(3):
                for s in range(2):
                    lr, li = left[s][a]
                    rr, ri = right[s][b]
                    re = lr * rr + li * ri
                    im = li * rr - lr * ri
                    old = out[a][b]
                    out[a][b] = (re, im) if old is None else (old[0] + re, old[1] + im)
        return out

    def finish(mu, t, heads):
        parts = []
        for q in range(2):
            ahead_x, ahead_y = heads(1 - q)
            here_y = project(load_spinor(W.at[q], t), mu, True)
            here_x = project(load_spinor(S.at[q], t), mu, False)
            out = [[None] * 3 for _ in range(3)]
            out = outer_into(out, ahead_x, here_y)
            parts.append(outer_into(out, ahead_y, here_x))
        both, link = [], []
        for a in range(3):
            line, link_line = [], []
            for b in range(3):
                pair, link_pair = [], []
                for ri in range(2):
                    zero, one = parts[0][a][b][ri], parts[1][a][b][ri]
                    copy_one = pltpu.roll(merge(t, zero, one, 1), 1, 1)
                    copy_zero = merge(t, zero, one, 0)
                    pair.append(copy_zero + copy_one if ri == 0 else copy_zero - copy_one)
                    link_pair.append(merge(t, L[0, ri, mu, a, b, t], L[1, ri, mu, a, b, t], 0))
                line.append(pair)
                link_line.append(link_pair)
            both.append(line)
            link.append(link_line)
        merged = []
        for a in range(3):
            line = []
            for b in range(3):
                re = im = None
                for k in range(3):
                    lr, li = link[a][k]
                    br, bi = both[k][b]
                    tr, ti = lr * br - li * bi, lr * bi + li * br
                    re = tr if re is None else re + tr
                    im = ti if im is None else im + ti
                line.append((re, im))
            merged.append(line)
        trace = merged[0][0][1] + merged[1][1][1] + merged[2][2][1]
        third = trace * (1.0 / 3.0)
        photon[mu, t] = CHARGE * trace
        for a in range(3):
            force[0, mu, a, a, t] = jnp.zeros_like(trace)
            force[1, mu, a, a, t] = merged[a][a][1] - third
            for b in range(a + 1, 3):
                re = 0.5 * (merged[a][b][0] - merged[b][a][0])
                im = 0.5 * (merged[a][b][1] + merged[b][a][1])
                force[0, mu, a, b, t] = re
                force[0, mu, b, a, t] = -re
                force[1, mu, a, b, t] = im
                force[1, mu, b, a, t] = im

    def force_z(t):
        finish(3, t, lambda p: (z_ahead(project(load_spinor(S.at[p], t), 3, True)),
                                z_ahead(project(load_spinor(W.at[p], t), 3, False))))

    over_t(force_z)

    def force_t(t):
        finish(0, t, lambda p: (project(load_spinor(S.at[p], t + 1), 0, True),
                                project(load_spinor(W.at[p], t + 1), 0, False)))

    if nt > 1:
        over_t(force_t, nt - 1)

    numbers = [2 * rounds + (p + rounds) % 2 for p in range(2)]
    for k in (2, 1, 0):
        for p in range(2):
            force_copy(k, p).wait()
            copy_of(2 * k, numbers[p]).wait()
        if k == 0:
            finish(0, nt - 1, lambda p: (load_half(frecv[0].at[p]),
                                         load_half(recv[0].at[numbers[p] % 4])))
        else:
            def force_k(t):
                finish(k, t, lambda p: (
                    shifted(project(load_spinor(S.at[p], t), k, True), frecv[k].at[p],
                            k, 1 - p, t, True),
                    shifted(project(load_spinor(W.at[p], t), k, False),
                            recv[2 * k].at[numbers[p] % 4], k, 1 - p, t, True)))
            over_t(force_k)


def per_device(source, gauge_links, photon_angles):
    _, _, _, copies, nt, nx, ny, nz = source.shape
    R = nx * ny
    face = [(2, 2, 3, R, nz),
            (2, 3, -(-2 * nt // nx), R, nz),
            (2, 3, -(-2 * nt // ny), R, nz)]
    f32 = jnp.float32
    field = (2, 2, 4, 3, nt, R, nz)

    def vm(shape):
        return pltpu.VMEM(shape, f32)

    color, photon = pl.pallas_call(
        functools.partial(kernel, (copies, nt, nx, ny, nz)),
        out_shape=(jax.ShapeDtypeStruct((2, 4, 3, 3, nt, R, nz), f32),
                   jax.ShapeDtypeStruct((4, nt, R, nz), f32)),
        in_specs=[pl.BlockSpec(memory_space=pltpu.VMEM)] * 3,
        out_specs=(pl.BlockSpec(memory_space=pltpu.VMEM),) * 2,
        scratch_shapes=[
            vm((2, 2, 4, 3, 3, nt, R, nz)),
            vm(field),
            vm((2,) + field),
            vm((2, 2, 2, 2, 3, nt, R, nz)),
            [vm((2,) + face[kind // 2]) for kind in range(6)],
            [vm((4,) + face[kind // 2]) for kind in range(6)],
            [vm((2,) + face[k]) for k in range(3)],
            [vm((2,) + face[k]) for k in range(3)],
            pltpu.SemaphoreType.DMA((6, 2)),
            pltpu.SemaphoreType.DMA((6, 4)),
            pltpu.SemaphoreType.DMA((3, 2)),
            pltpu.SemaphoreType.DMA((3, 2)),
        ],
        compiler_params=pltpu.CompilerParams(
            collective_id=0, has_side_effects=True, vmem_limit_bytes=40 * 1024 * 1024),
    )(source.reshape(2, 4, 3, copies, nt, R, nz),
      gauge_links.reshape(2, 4, 3, 3, nt, R, nz),
      photon_angles.reshape(4, nt, R, nz))
    return (color.reshape(2, 4, 3, 3, nt, nx, ny, nz), photon.reshape(4, nt, nx, ny, nz))


def solution(mesh):
    in_specs = (
        P(None, None, None, None, "ta", "gx", "yz", None),
        P(None, None, None, None, "ta", "gx", "yz", None),
        P(None, "ta", "gx", "yz", None),
    )
    out_specs = (P(None, None, None, None, "ta", "gx", "yz", None), P(None, "ta", "gx", "yz", None))
    return jax.shard_map(
        per_device, mesh=mesh, in_specs=in_specs, out_specs=out_specs, check_vma=False
    )
```

time: 63.4 us -> 56.8 us (0.90)
  Pallas kernels: 57.9 us -> 51.7 us
    pallas_call x1, Pallas kernels: 57.9 us -> 51.7 us  [per_device(): pl.pallas_call(functools.partial(kernel, (copies, nt, nx, ny, nz)), out_s...]
where the time goes in v1:
time: 56.8 us; the launch traced here: 56.5 us
  Pallas kernels  51.7 us (91%)
  local copies, waits for them, and re-layouts  4.24 us (7%)
  between operations  0.65 us (1%)
    pallas_call x1, Pallas kernels, per_device(): pl.pallas_call(functools.partial(kernel, (copies, nt, nx, ny, nz)), out_s...  51.7 us
    unnamed x8, local copies, waits for them, and re-layouts  4.24 us

profile of v1, /device:TPU:0, one launch (start us, length us, event | category | flops | bytes accessed | tf_op | source)
XLA Modules:
  0.0 56.5 jit_solution(7259356457529821084)
XLA Ops:
  0.6 0.0 copy-start
  0.6 1.1 %copy-done = f32[2,4,3,3,2,2,4,128]{7,6,5,4,3,2,1,0:T(4,128)S(1)} copy-done((f32[2,4,3,3,2,2,4,128]{7,6,5,4,3,2,1,0:T(4,128)S(1)}, f32[2,4,3,3,2,2,4,128]{7,6,5,4,3,2,1,0:T(4,128)}, u32[]{:S(2)}) %copy-start) | copy-done | bytes 589848
  1.7 0.0 copy-start.1
  1.7 1.0 %copy-done.1 = f32[2,4,3,2,2,2,4,128]{7,6,5,4,3,2,1,0:T(4,128)S(1)} copy-done((f32[2,4,3,2,2,2,4,128]{7,6,5,4,3,2,1,0:T(4,128)S(1)}, f32[2,4,3,2,2,2,4,128]{7,6,5,4,3,2,1,0:T(4,128)}, u32[]{:S(2)}) %copy-start.1) | copy-done | bytes 393240
  2.7 0.0 copy-start.2
  2.7 0.8 %copy-done.2 = f32[4,2,2,4,128]{4,3,2,1,0:T(4,128)S(1)} copy-done((f32[4,2,2,4,128]{4,3,2,1,0:T(4,128)S(1)}, f32[4,2,2,4,128]{4,3,2,1,0:T(4,128)}, u32[]{:S(2)}) %copy-start.2) | copy-done | bytes 32792
  3.5 51.7 %shard_map.50 = (f32[2,4,3,3,2,8,128]{6,5,4,3,2,1,0:T(8,128)S(1)}, f32[4,2,8,128]{3,2,1,0:T(8,128)S(1)}) custom-call(f32[2,4,3,2,2,8,128]{6,5,4,3,2,1,0:T(8,128)S(1)} %bitcast.7, f32[2,4,3,3,2,8,128]{6,5,4,3,2,1,0:T(8,128)S(1)} %bitcast.5, f32[4,2,8,128]{3,2,1,0:T(8,128)S(1)} %bitcast.8), custom_call_target="tpu_custom_call" | custom-call | tf_op jit(solution)/shard_map/pallas_call | solution.py:495
  55.1 0.8 %copy.7 = f32[2,4,3,3,2,2,4,128]{7,6,5,4,3,2,1,0:T(4,128)} copy(f32[2,4,3,3,2,2,4,128]{7,6,5,4,3,2,1,0:T(4,128)S(1)} %bitcast.6) | data formatting | bytes 1179648
  55.9 0.6 %copy.8 = f32[4,2,2,4,128]{4,3,2,1,0:T(4,128)} copy(f32[4,2,2,4,128]{4,3,2,1,0:T(4,128)S(1)} %bitcast.9) | data formatting | bytes 65536
Async XLA Ops:
  0.6 1.1 %copy-start = (f32[2,4,3,3,2,2,4,128]{7,6,5,4,3,2,1,0:T(4,128)S(1)}, f32[2,4,3,3,2,2,4,128]{7,6,5,4,3,2,1,0:T(4,128)}, u32[]{:S(2)}) copy-start(f32[2,4,3,3,2,2,4,128]{7,6,5,4,3,2,1,0:T(4,128)} %param.4) | copy-start | bytes 1769476
  1.7 1.0 %copy-start.1 = (f32[2,4,3,2,2,2,4,128]{7,6,5,4,3,2,1,0:T(4,128)S(1)}, f32[2,4,3,2,2,2,4,128]{7,6,5,4,3,2,1,0:T(4,128)}, u32[]{:S(2)}) copy-start(f32[2,4,3,2,2,2,4,128]{7,6,5,4,3,2,1,0:T(4,128)} %param.3) | copy-start | bytes 1179652
  2.7 0.8 %copy-start.2 = (f32[4,2,2,4,128]{4,3,2,1,0:T(4,128)S(1)}, f32[4,2,2,4,128]{4,3,2,1,0:T(4,128)}, u32[]{:S(2)}) copy-start(f32[4,2,2,4,128]{4,3,2,1,0:T(4,128)} %param.5) | copy-start | bytes 98308

commit v2 on v1

--- a/solution.py
+++ b/solution.py
@@ -377,7 +377,14 @@
                     pack(fsend[k].at[q], project(spinor, k, True), k, t, True)
 
             over_t(face)
-            for k in range(3):
+        @pl.when(n == DEGREE + 1)
+        def _():
+            for k in (1, 2):
+                force_copy(k, q).start()
+
+        @pl.when(n == rounds - 1)
+        def _():
+            for k in (0,):
                 force_copy(k, q).start()
 
         return carry

time: 56.8 us -> 55.3 us (0.974)
  Pallas kernels: 51.7 us -> 50.2 us
    pallas_call x1, Pallas kernels: 51.7 us -> 50.2 us  [per_device(): pl.pallas_call(functools.partial(kernel, (copies, nt, nx, ny, nz)), out_s...]
where the time goes in v2:
time: 55.3 us; the launch traced here: 55.1 us
  Pallas kernels  50.2 us (91%)
  local copies, waits for them, and re-layouts  4.24 us (8%)
  between operations  0.65 us (1%)
    pallas_call x1, Pallas kernels, per_device(): pl.pallas_call(functools.partial(kernel, (copies, nt, nx, ny, nz)), out_s...  50.2 us
    unnamed x8, local copies, waits for them, and re-layouts  4.24 us

profile of v2, /device:TPU:0, one launch (start us, length us, event | category | flops | bytes accessed | tf_op | source)
XLA Modules:
  0.0 55.1 jit_solution(9635429682840344247)
XLA Ops:
  0.6 0.0 copy-start
  0.6 1.1 %copy-done = f32[2,4,3,3,2,2,4,128]{7,6,5,4,3,2,1,0:T(4,128)S(1)} copy-done((f32[2,4,3,3,2,2,4,128]{7,6,5,4,3,2,1,0:T(4,128)S(1)}, f32[2,4,3,3,2,2,4,128]{7,6,5,4,3,2,1,0:T(4,128)}, u32[]{:S(2)}) %copy-start) | copy-done | bytes 589848
  1.7 0.0 copy-start.1
  1.7 1.0 %copy-done.1 = f32[2,4,3,2,2,2,4,128]{7,6,5,4,3,2,1,0:T(4,128)S(1)} copy-done((f32[2,4,3,2,2,2,4,128]{7,6,5,4,3,2,1,0:T(4,128)S(1)}, f32[2,4,3,2,2,2,4,128]{7,6,5,4,3,2,1,0:T(4,128)}, u32[]{:S(2)}) %copy-start.1) | copy-done | bytes 393240
  2.7 0.0 copy-start.2
  2.7 0.8 %copy-done.2 = f32[4,2,2,4,128]{4,3,2,1,0:T(4,128)S(1)} copy-done((f32[4,2,2,4,128]{4,3,2,1,0:T(4,128)S(1)}, f32[4,2,2,4,128]{4,3,2,1,0:T(4,128)}, u32[]{:S(2)}) %copy-start.2) | copy-done | bytes 32792
  3.5 50.2 %shard_map.50 = (f32[2,4,3,3,2,8,128]{6,5,4,3,2,1,0:T(8,128)S(1)}, f32[4,2,8,128]{3,2,1,0:T(8,128)S(1)}) custom-call(f32[2,4,3,2,2,8,128]{6,5,4,3,2,1,0:T(8,128)S(1)} %bitcast.7, f32[2,4,3,3,2,8,128]{6,5,4,3,2,1,0:T(8,128)S(1)} %bitcast.5, f32[4,2,8,128]{3,2,1,0:T(8,128)S(1)} %bitcast.8), custom_call_target="tpu_custom_call" | custom-call | tf_op jit(solution)/shard_map/pallas_call | solution.py:502
  53.6 0.8 %copy.7 = f32[2,4,3,3,2,2,4,128]{7,6,5,4,3,2,1,0:T(4,128)} copy(f32[2,4,3,3,2,2,4,128]{7,6,5,4,3,2,1,0:T(4,128)S(1)} %bitcast.6) | data formatting | bytes 1179648
  54.5 0.6 %copy.8 = f32[4,2,2,4,128]{4,3,2,1,0:T(4,128)} copy(f32[4,2,2,4,128]{4,3,2,1,0:T(4,128)S(1)} %bitcast.9) | data formatting | bytes 65536
Async XLA Ops:
  0.6 1.1 %copy-start = (f32[2,4,3,3,2,2,4,128]{7,6,5,4,3,2,1,0:T(4,128)S(1)}, f32[2,4,3,3,2,2,4,128]{7,6,5,4,3,2,1,0:T(4,128)}, u32[]{:S(2)}) copy-start(f32[2,4,3,3,2,2,4,128]{7,6,5,4,3,2,1,0:T(4,128)} %param.4) | copy-start | bytes 1769476
  1.7 1.0 %copy-start.1 = (f32[2,4,3,2,2,2,4,128]{7,6,5,4,3,2,1,0:T(4,128)S(1)}, f32[2,4,3,2,2,2,4,128]{7,6,5,4,3,2,1,0:T(4,128)}, u32[]{:S(2)}) copy-start(f32[2,4,3,2,2,2,4,128]{7,6,5,4,3,2,1,0:T(4,128)} %param.3) | copy-start | bytes 1179652
  2.7 0.8 %copy-start.2 = (f32[4,2,2,4,128]{4,3,2,1,0:T(4,128)S(1)}, f32[4,2,2,4,128]{4,3,2,1,0:T(4,128)}, u32[]{:S(2)}) copy-start(f32[4,2,2,4,128]{4,3,2,1,0:T(4,128)} %param.5) | copy-start | bytes 98308
